TPU v7x, 32 devices: a whole 2x2x4 slice. The times are simulated.
32 devices in a mesh: row: 16 (over z, x, core), col: 2 (over y).
Axes of the slice: x: 2, y: 2, z: 4, core: 2. Of those that a mesh axis runs over, the one named last changes fastest.
Arguments:
- gbar: float32 [8192, 8192], P('row', 'col'), may hold values from -9 to 9
- panels: float32 [8192, 1024], P('row'), may hold values from -0.0625 to 0.0625
- panel_cot: float32 [8192, 1024], P('row'), may hold values from -6 to 6
- inverses: float32 [2, 512, 512], replicated, may hold values from -1 to 2, as said below
Outputs:
- adjoint: float32 [8192, 1024], P('row')
- diag_adjoint: float32 [2, 512, 512], P(None, 'row')
Inputs may be any that keep to these rules, and one draw needn't show every extreme that they name: Each inverses[i] is lower triangular with diagonal entries between 1 and 2.
All inputs are finite; a program needn't handle non-finite values.
Results may differ from a plain program's by a relative error of at most 0.000071.
Values sent between devices are 32-bit elements; how exact they have to be, the bound alone decides.
A program may use at most 128 MiB of HBM per device.

v0:
```python
import jax
import jax.numpy as jnp
from jax import lax
from jax.sharding import PartitionSpec as P


def spread(value, axis, source):
    kept = jnp.where(lax.axis_index(axis) == source, value, 0).astype(value.dtype)
    return lax.psum(kept, axis)


def per_device(gbar, panels, panel_cot, inverses):
    width = inverses.shape[-1]
    exact_mode = lax.Precision.HIGHEST
    row_id = lax.axis_index("row")
    col_count = lax.axis_size("col")
    partial_value = lax.dot_general(
        gbar,
        panels,
        (((0,), (0,)), ((), ())),
        precision=exact_mode,
        preferred_element_type=jnp.float32,
    )
    summed = lax.psum(partial_value, "row")
    own_tile = lax.dynamic_slice_in_dim(summed, row_id // col_count * width, width, 0)
    coupled = spread(own_tile, "col", row_id % col_count)
    combined = panel_cot - 2.0 * coupled
    first_adj = jnp.dot(
        combined[:, :width], inverses[0], precision=exact_mode, preferred_element_type=jnp.float32
    )
    second_adj = jnp.dot(
        combined[:, width:], inverses[1], precision=exact_mode, preferred_element_type=jnp.float32
    )
    adjoint = jnp.concatenate([first_adj, second_adj], axis=1)
    contract = (((0,), (0,)), ((), ()))
    first_diag = -lax.dot_general(
        first_adj,
        panels[:, :width],
        contract,
        precision=exact_mode,
        preferred_element_type=jnp.float32,
    )
    second_diag = -lax.dot_general(
        second_adj,
        panels[:, width:],
        contract,
        precision=exact_mode,
        preferred_element_type=jnp.float32,
    )
    diag_terms = jnp.stack([first_diag, second_diag])
    diag_adjoint = lax.psum_scatter(diag_terms, "row", scatter_dimension=1, tiled=True)
    return (adjoint, diag_adjoint)


def solution(mesh):
    in_specs = (P("row", "col"), P("row", None), P("row", None), P())
    out_specs = (P("row", None), P(None, "row", None))
    return jax.shard_map(
        per_device, mesh=mesh, in_specs=in_specs, out_specs=out_specs, check_vma=False
    )
```

profile of v0, /device:TPU:0, one launch (start us, length us, event | category | flops | bytes accessed | tf_op | source)
XLA Modules:
  0.0 485.4 jit_solution(16080054003184823967)
XLA Ops:
  7.2 0.0 all-reduce.3.cloned.1.call-start
  7.2 31.4 %fusion.12 = f32[4096,1024]{1,0:T(8,128)} fusion(f32[512,4096]{1,0:T(8,128)} %param.4, f32[512,1024]{1,0:T(8,128)} %param.5), kind=kOutput, calls=%fused_computation.18 | convolution fusion | flops 25769803776 | bytes 27262976 | tf_op jit(solution)/shard_map/dot_general | solution.py:17
  38.6 0.0 all-reduce.3.cloned.1.call-update
  38.6 0.0 all-reduce.5.cloned.1.call-start
  38.7 301.0 %all-reduce.3.cloned.1.call-done = f32[4096,1024]{1,0:T(8,128)} async-done(((f32[4096,1024]{1,0:T(8,128)}), f32[4096,1024]{1,0:T(8,128)}) %all-reduce.3.cloned.1.call-update) | async-done | bytes 16777232 | tf_op jit(solution)/shard_map/psum | solution.py:24
  339.8 3.2 dynamic-slice_select_fusion
  343.0 0.0 copy-start.1
  343.0 0.0 all-reduce.5.cloned.1.call-update
  343.0 0.2 reduce-scatter.2.cloned.1.call-start
  343.2 62.6 %all-reduce.5.cloned.1.call-done = f32[512,1024]{1,0:T(8,128)} async-done(((f32[512,1024]{1,0:T(8,128)}), f32[512,1024]{1,0:T(8,128)}) %all-reduce.5.cloned.1.call-update) | async-done | bytes 2097168 | tf_op jit(solution)/shard_map/psum | solution.py:9
  405.8 0.0 copy-done.1
  405.8 0.0 copy-start.2
  405.8 2.2 multiply_subtract_fusion
  408.0 0.1 copy-done.2
  408.0 1.9 fusion.2
  409.9 0.0 copy-start
  410.0 1.9 fusion.4
  411.9 0.0 copy-done
  411.9 1.9 fusion
  413.7 1.9 fusion.1
  415.6 1.5 pad_maximum_fusion.1
  417.1 0.0 reduce-scatter.2.cloned.1.call-update
  417.1 1.5 pad_maximum_fusion
  418.6 2.9 copy.6
  421.5 57.3 %reduce-scatter.2.cloned.1.call-done = f32[2,32,512]{2,1,0:T(8,128)} async-done(((f32[2,512,512]{2,1,0:T(8,128)}), f32[2,32,512]{2,1,0:T(8,128)}) %reduce-scatter.2.cloned.1.call-update) | async-done | bytes 131088 | tf_op jit(solution)/shard_map/reduce_scatter | solution.py:51
Async XLA Ops:
  7.2 332.6 %all-reduce.3.cloned.1.call-start = ((), (), s32[]{:S(2)}) async-start(), calls=%async_computation.1 | async-start | bytes 33554432 | tf_op jit(solution)/shard_map/psum | solution.py:24
  38.6 367.2 %all-reduce.5.cloned.1.call-start = ((), (), s32[]{:S(2)}) async-start(), calls=%async_computation.2 | async-start | bytes 4194304 | tf_op jit(solution)/shard_map/psum | solution.py:9
  343.0 62.9 %copy-start.1 = (f32[512,1024]{1,0:T(8,128)S(1)}, f32[512,1024]{1,0:T(8,128)}, u32[]{:S(2)}) copy-start(f32[512,1024]{1,0:T(8,128)} %param.6) | copy-start | bytes 6291460
  343.0 135.9 %reduce-scatter.2.cloned.1.call-start = ((), (), s32[]{:S(2)}) async-start(), calls=%async_computation.3 | async-start | bytes 2228224 | tf_op jit(solution)/shard_map/reduce_scatter | solution.py:51
  405.8 2.2 copy-start.2
  409.9 1.9 copy-start
Sparse Core Ops, SparseCore 0:
  38.8 300.9 all-reduce.2
  343.1 62.6 all-reduce.4
  417.3 61.5 reduce-scatter.1
where the time goes:
time: 486 us; the launch traced here: 485 us
  waiting for transfers between devices  421 us (87%)
  matrix products  38.9 us (8%)
  between operations  13.8 us (3%)
  other arithmetic  8.34 us (2%)
    psum x1, waiting for transfers between devices, per_device(): summed = lax.psum(partial_value, 'row')  301 us
    psum x1, waiting for transfers between devices, spread(): return lax.psum(kept, axis)  62.6 us
    reduce_scatter x1, waiting for transfers between devices, per_device(): lax.psum_scatter(diag_terms, 'row', scatter_dimension=1, tiled=True)  57.3 us
    dot_general x1, matrix products, per_device(): lax.dot_general(gbar, panels, (((0,), (0,)), ((), ())), precision=exact_m...  31.4 us
  transfers between devices with their start and end apart: 3, of which 3 were waited for; matrix products, arithmetic and copies ran while one was open for 1% of the time, Pallas kernels for 0%

commit v1 on v0

v1 whole, which is shorter than its diff:
```python
import jax
import jax.numpy as jnp
from jax import lax
from jax.experimental import pallas as pl
from jax.experimental.pallas import tpu as pltpu
from jax.sharding import PartitionSpec as P

MESH = pl.DeviceIdType.MESH
SUBS = 2


def halves(value):
    high = value.astype(jnp.bfloat16)
    low = (value - high.astype(jnp.float32)).astype(jnp.bfloat16)
    return high, low


def product(left, right):
    (left_high, left_low), (right_high, right_low) = left, right

    def one(a, b):
        return jnp.dot(a, b, preferred_element_type=jnp.float32)

    return one(left_high, right_low) + one(left_low, right_high) + one(left_high, right_high)


def ring_kernel(
    chips, gbar, panels, cot, inverses,
    adjoint, diag,
    g_v, p_v, cot_v, inv_v, p_high, p_low, terms, other, arrived, final, adj_v, diag_v,
    load_sems, out_sems, pair_send, pair_recv, ring_send, ring_recv, end_send, end_recv,
):
    width = inverses.shape[-1]
    lane = width // 4
    piece = lane // SUBS
    row = lax.axis_index("row")
    col = lax.axis_index("col")
    chip = row // 2
    core = row % 2
    mate = 1 - core
    half = chips // 2

    def place_of(chip_id):
        return jnp.where(chip_id % 2 == 0, chip_id // 2, chips - 1 - chip_id // 2)

    def chip_at(place):
        return jnp.where(place < half, 2 * place, 2 * (chips - 1 - place) + 1)

    place = place_of(chip)
    right = chip_at((place + 1) % chips)
    left = chip_at((place + chips - 1) % chips)

    def tile_at(way, step):
        ahead = jnp.where(way == 0, place + 2 * chips - 1 - step, place + 1 + step)
        return chip_at(ahead % chips)

    def load_g(tile):
        start = pl.multiple_of(tile * width, width)
        return pltpu.make_async_copy(gbar.at[:, pl.ds(start, width)], g_v.at[tile], load_sems.at[tile])

    load_p = pltpu.make_async_copy(panels, p_v, load_sems.at[chips])
    load_cot = pltpu.make_async_copy(cot, cot_v, load_sems.at[chips + 1])
    load_inv = pltpu.make_async_copy(inverses, inv_v, load_sems.at[chips + 2])
    load_p.start()
    for hop in (1, 2, 3):
        load_g(chip_at((place + chips - hop) % chips)).start()
        load_g(chip_at((place + hop) % chips)).start()
    load_g(chip_at((place + half) % chips)).start()
    load_g(chip).start()
    load_cot.start()
    load_inv.start()

    barrier = pltpu.get_barrier_semaphore()
    friends = [
        (2 * right + core, col),
        (2 * left + core, col),
        (2 * chip + mate, col),
        (2 * chip + core, 1 - col),
        (2 * chip + mate, 1 - col),
    ]
    for friend in friends:
        pl.semaphore_signal(barrier, inc=1, device_id=friend, device_id_type=MESH)

    load_p.wait()
    for block in range(4):
        rows = slice(block * width // 2, (block + 1) * width // 2)
        high, low = halves(p_v[:, rows].T)
        p_high[rows, :] = high
        p_low[rows, :] = low

    def pair_copy(panel, way, step):
        return pltpu.make_async_remote_copy(
            terms.at[panel, way, step, mate],
            other.at[panel, way, step],
            pair_send.at[panel, way, step],
            pair_recv.at[panel, way, step],
            device_id=(2 * chip + mate, col),
            device_id_type=MESH,
        )

    def ring_copy(panel, way, step, sub):
        target = jnp.where(way == 0, right, left)
        rows = pl.ds(sub * piece, piece)
        return pltpu.make_async_remote_copy(
            terms.at[panel, way, step, core, rows],
            arrived.at[panel, way, step, rows],
            ring_send.at[panel, way, step, sub],
            ring_recv.at[panel, way, step, sub],
            device_id=(2 * target + core, col),
            device_id_type=MESH,
        )

    def end_copy(panel, way, plane, source_core):
        return pltpu.make_async_remote_copy(
            terms.at[panel, way, chips - 1, source_core],
            final.at[panel, way, source_core],
            end_send.at[panel, way, plane],
            end_recv.at[panel, way, source_core],
            device_id=(2 * chip + col, jnp.where(plane == 0, col, 1 - col)),
            device_id_type=MESH,
        )

    def end_local(panel, way, source_core):
        return pltpu.make_async_copy(
            terms.at[panel, way, chips - 1, source_core],
            final.at[panel, way, source_core],
            end_recv.at[panel, way, source_core],
        )

    def make_terms(count):
        panel, step = count // chips, count % chips
        for way in (0, 1):
            tile = tile_at(way, step)

            @pl.when((panel == 0) & (step < half if way == 0 else step < half - 1))
            def _():
                load_g(tile).wait()

            @pl.when((panel == 0) & (step == chips - 1) & (way == 0))
            def _():
                load_g(tile).wait()

            rows = pl.ds(pl.multiple_of(panel * width + way * (width // 2), width // 2), width // 2)
            value = product((p_high[rows, :], p_low[rows, :]), halves(g_v[tile]))
            terms[panel, way, step, 0] = value[:lane]
            terms[panel, way, step, 1] = value[lane:]
            pair_copy(panel, way, step).start()

    def ring_step(count):
        panel, step = count // chips, count % chips
        for way in (0, 1):
            pair_copy(panel, way, step).wait_recv()
        for sub in range(SUBS):
            rows = pl.ds(sub * piece, piece)
            for way in (0, 1):
                @pl.when(step > 0)
                def _():
                    ring_copy(panel, way, step - 1, sub).wait_recv()
                    terms[panel, way, step, core, rows] = (
                        terms[panel, way, step, core, rows]
                        + other[panel, way, step, rows]
                        + arrived[panel, way, step - 1, rows]
                    )

                @pl.when(step == 0)
                def _():
                    terms[panel, way, step, core, rows] = (
                        terms[panel, way, step, core, rows] + other[panel, way, step, rows]
                    )

                @pl.when(step < chips - 1)
                def _():
                    ring_copy(panel, way, step, sub).start()

        @pl.when(step == chips - 1)
        def _():
            for way in (0, 1):
                end_copy(panel, way, 1, core).start()

                @pl.when(core == col)
                def _():
                    end_local(panel, way, core).start()

                @pl.when(core != col)
                def _():
                    end_copy(panel, way, 0, core).start()

    def finish(panel):
        for way in (0, 1):
            for source in (0, 1):
                end_local(panel, way, source).wait()
        columns = slice(panel * width, (panel + 1) * width)
        coupled = final[panel].reshape(width, width)
        combined = cot_v[:, columns].T - 2.0 * coupled
        turned = product(halves(inv_v[panel].T), halves(combined))
        adj_v[:, columns] = turned.T
        own = (p_v[:, columns])
        diag_v[panel] = -product(halves(turned), halves(own))
        pltpu.make_async_copy(adj_v.at[:, columns], adjoint.at[:, columns], out_sems.at[0, panel]).start()
        pltpu.make_async_copy(diag_v.at[panel], diag.at[panel], out_sems.at[1, panel]).start()

    pl.semaphore_wait(barrier, len(friends))
    make_terms(jnp.int32(0))
    load_cot.wait()
    load_inv.wait()

    def body(count, carry):
        @pl.when(count < 2 * chips - 1)
        def _():
            make_terms(count + 1)

        ring_step(count)

        @pl.when(count == chips + 2)
        def _():
            finish(0)

        return carry

    lax.fori_loop(0, 2 * chips, body, 0)
    finish(1)

    def drain(count, carry):
        panel, step = count // chips, count % chips
        for way in (0, 1):
            pair_copy(panel, way, step).wait_send()

            @pl.when(step < chips - 1)
            def _():
                for sub in range(SUBS):
                    ring_copy(panel, way, step, sub).wait_send()

        return carry

    lax.fori_loop(0, 2 * chips, drain, 0)
    for panel in (0, 1):
        columns = slice(panel * width, (panel + 1) * width)
        for way in (0, 1):
            end_copy(panel, way, 1, core).wait_send()

            @pl.when(core != col)
            def _():
                end_copy(panel, way, 0, core).wait_send()

        pltpu.make_async_copy(adj_v.at[:, columns], adjoint.at[:, columns], out_sems.at[0, panel]).wait()
        pltpu.make_async_copy(diag_v.at[panel], diag.at[panel], out_sems.at[1, panel]).wait()


def ring_device(gbar, panels, panel_cot, inverses):
    width = inverses.shape[-1]
    chips = lax.axis_size("row") // 2
    lane = width // 4
    f32, dma = jnp.float32, pltpu.SemaphoreType.DMA
    anywhere = pl.BlockSpec(memory_space=pl.ANY)

    def kernel(*refs):
        ring_kernel(chips, *refs)

    adjoint, diag_terms = pl.pallas_call(
        kernel,
        out_shape=(
            jax.ShapeDtypeStruct(panels.shape, f32),
            jax.ShapeDtypeStruct(inverses.shape, f32),
        ),
        in_specs=[anywhere] * 4,
        out_specs=(anywhere, anywhere),
        scratch_shapes=[
            pltpu.VMEM((chips, width, width), f32),
            pltpu.VMEM(panels.shape, f32),
            pltpu.VMEM(panels.shape, f32),
            pltpu.VMEM(inverses.shape, f32),
            pltpu.VMEM((2 * width, width), jnp.bfloat16),
            pltpu.VMEM((2 * width, width), jnp.bfloat16),
            pltpu.VMEM((2, 2, chips, 2, lane, width), f32),
            pltpu.VMEM((2, 2, chips, lane, width), f32),
            pltpu.VMEM((2, 2, chips - 1, lane, width), f32),
            pltpu.VMEM((2, 2, 2, lane, width), f32),
            pltpu.VMEM(panels.shape, f32),
            pltpu.VMEM(inverses.shape, f32),
            dma((chips + 3,)),
            dma((2, 2)),
            dma((2, 2, chips)),
            dma((2, 2, chips)),
            dma((2, 2, chips - 1, SUBS)),
            dma((2, 2, chips - 1, SUBS)),
            dma((2, 2, 2)),
            dma((2, 2, 2)),
        ],
        compiler_params=pltpu.CompilerParams(
            collective_id=0, has_side_effects=True, vmem_limit_bytes=62 * 1024 * 1024
        ),
    )(gbar, panels, panel_cot, inverses)
    diag_adjoint = lax.psum_scatter(diag_terms, "row", scatter_dimension=1, tiled=True)
    return adjoint, diag_adjoint


def plain_device(gbar, panels, panel_cot, inverses):
    width = inverses.shape[-1]
    mode = lax.Precision.HIGHEST
    row_id = lax.axis_index("row")
    col_count = lax.axis_size("col")
    contract = (((0,), (0,)), ((), ()))
    partial_value = lax.dot_general(
        gbar, panels, contract, precision=mode, preferred_element_type=jnp.float32
    )
    summed = lax.psum(partial_value, "row")
    own_tile = lax.dynamic_slice_in_dim(summed, row_id // col_count * width, width, 0)
    own_tile = jnp.where(lax.axis_index("col") == row_id % col_count, own_tile, 0)
    combined = panel_cot - 2.0 * lax.psum(own_tile, "col")
    adjoint, terms = [], []
    for panel in (0, 1):
        columns = slice(panel * width, (panel + 1) * width)
        adjoint.append(
            jnp.dot(combined[:, columns], inverses[panel], precision=mode, preferred_element_type=jnp.float32)
        )
        terms.append(
            -lax.dot_general(
                adjoint[-1], panels[:, columns], contract, precision=mode, preferred_element_type=jnp.float32
            )
        )
    diag_adjoint = lax.psum_scatter(jnp.stack(terms), "row", scatter_dimension=1, tiled=True)
    return jnp.concatenate(adjoint, axis=1), diag_adjoint


def solution(mesh):
    in_specs = (P("row", "col"), P("row", None), P("row", None), P())
    out_specs = (P("row", None), P(None, "row", None))
    on_ring = mesh.shape["col"] == 2 and mesh.shape["row"] == 16
    return jax.shard_map(
        ring_device if on_ring else plain_device,
        mesh=mesh, in_specs=in_specs, out_specs=out_specs, check_vma=False,
    )
```

time: 486 us -> 186 us (0.38)
  waiting for transfers between devices: 421 us -> 67.3 us
  Pallas kernels: 0 us -> 103 us
  matrix products: 38.9 us -> 0 us
  other arithmetic: 8.34 us -> 0 us
    psum x2 -> x0, waiting for transfers between devices: 364 us -> none  [the longest x1 301 us: per_device(): summed = lax.psum(partial_value, 'row')]
    pallas_call x0 -> x1, Pallas kernels: none -> 103 us  [ring_device(): pl.pallas_call(kernel, out_shape=(jax.ShapeDtypeStruct(panels.shape, f32)...]
    dot_general x5 -> x0, matrix products: 38.9 us -> none  [the longest x1 31.4 us: per_device(): lax.dot_general(gbar, panels, (((0,), (0,)), ((), ())), precision=exact_m...]
    reduce_scatter x1, waiting for transfers between devices: 57.3 us -> 67.2 us  [ring_device(): lax.psum_scatter(diag_terms, 'row', scatter_dimension=1, tiled=True)]
  transfers between devices with their start and end apart: 3 -> 1, of which waited for: 3 -> 1; matrix products, arithmetic and copies ran while one was open for 1% -> 0% of each run, Pallas kernels for 0% -> 0%
where the time goes in v1:
time: 186 us; the launch traced here: 185 us
  Pallas kernels  103 us (55%)
  waiting for transfers between devices  67.3 us (36%)
  between operations  14 us (8%)
    pallas_call x1, Pallas kernels, ring_device(): pl.pallas_call(kernel, out_shape=(jax.ShapeDtypeStruct(panels.shape, f32)...  103 us
    reduce_scatter x1, waiting for transfers between devices, ring_device(): lax.psum_scatter(diag_terms, 'row', scatter_dimension=1, tiled=True)  67.2 us
  transfers between devices with their start and end apart: 1, of which 1 were waited for; matrix products, arithmetic and copies ran while one was open for 0% of the time, Pallas kernels for 0%

profile of v1, /device:TPU:0, one launch (start us, length us, event | category | flops | bytes accessed | tf_op | source)
XLA Modules:
  0.0 185.5 jit_solution(3235875066036002928)
XLA Ops:
  7.2 0.0 reduce-scatter.2.cloned.1.call-start
  7.2 102.8 %shard_map.59 = (f32[512,1024]{1,0:T(8,128)}, f32[2,512,512]{2,1,0:T(8,128)}) custom-call(f32[512,4096]{1,0:T(8,128)} %refs_0_.1, f32[512,1024]{1,0:T(8,128)} %refs_1_.1, f32[512,1024]{1,0:T(8,128)} %refs_2_.1, f32[2,512,512]{2,1,0:T(8,128)} %refs_3_.1), custom_call_target="tpu_custom_call" | custom-call | tf_op jit(solution)/shard_map/pallas_call | solution.py:259
  110.0 0.0 copy-start
  110.0 0.0 reduce-scatter.2.cloned.1.call-update
  110.0 67.2 %reduce-scatter.2.cloned.1.call-done = f32[2,32,512]{2,1,0:T(8,128)} async-done(((f32[2,512,512]{2,1,0:T(8,128)}), f32[2,32,512]{2,1,0:T(8,128)}) %reduce-scatter.2.cloned.1.call-update) | async-done | bytes 131088 | tf_op jit(solution)/shard_map/reduce_scatter | solution.py:293
  177.3 0.0 copy-done
  177.3 1.3 copy.7
Async XLA Ops:
  7.2 170.1 %reduce-scatter.2.cloned.1.call-start = ((), (), s32[]{:S(2)}) async-start(), calls=%async_computation.1 | async-start | bytes 2228224 | tf_op jit(solution)/shard_map/reduce_scatter | solution.py:293
  110.0 67.3 %copy-start = (f32[512,1024]{1,0:T(8,128)S(1)}, f32[512,1024]{1,0:T(8,128)}, u32[]{:S(2)}) copy-start(f32[512,1024]{1,0:T(8,128)} %get-tuple-element.8) | copy-start | bytes 6291460
Sparse Core Ops, SparseCore 0:
  110.2 67.0 reduce-scatter.1

commit v2 on v1

--- a/solution.py
+++ b/solution.py
@@ -27,8 +27,10 @@
 def ring_kernel(
     chips, gbar, panels, cot, inverses,
     adjoint, diag,
-    g_v, p_v, cot_v, inv_v, p_high, p_low, terms, other, arrived, final, adj_v, diag_v,
+    g_v, p_v, cot_t, inv_v, inv_high, inv_low, p_high, p_low, terms, other, arrived, final, adj_v,
+    diag_v, diag_mate, diag_parts, diag_out,
     load_sems, out_sems, pair_send, pair_recv, ring_send, ring_recv, end_send, end_recv,
+    mate_sems, part_send, part_recv, swap_sems,
 ):
     width = inverses.shape[-1]
     lane = width // 4
@@ -58,22 +60,26 @@
         start = pl.multiple_of(tile * width, width)
         return pltpu.make_async_copy(gbar.at[:, pl.ds(start, width)], g_v.at[tile], load_sems.at[tile])
 
-    load_p = pltpu.make_async_copy(panels, p_v, load_sems.at[chips])
-    load_cot = pltpu.make_async_copy(cot, cot_v, load_sems.at[chips + 1])
-    load_inv = pltpu.make_async_copy(inverses, inv_v, load_sems.at[chips + 2])
-    load_p.start()
+    def load_p(panel):
+        columns = slice(panel * width, (panel + 1) * width)
+        return pltpu.make_async_copy(
+            panels.at[:, columns], p_v.at[:, columns], load_sems.at[chips + panel]
+        )
+
+    load_cot = pltpu.make_async_copy(cot, adj_v, load_sems.at[chips + 2])
+    load_inv = pltpu.make_async_copy(inverses, inv_v, load_sems.at[chips + 3])
+    load_p(0).start()
     for hop in (1, 2, 3):
         load_g(chip_at((place + chips - hop) % chips)).start()
         load_g(chip_at((place + hop) % chips)).start()
     load_g(chip_at((place + half) % chips)).start()
     load_g(chip).start()
+    load_p(1).start()
     load_cot.start()
     load_inv.start()
 
     barrier = pltpu.get_barrier_semaphore()
-    friends = [
-        (2 * right + core, col),
-        (2 * left + core, col),
+    friends = [(2 * ((chip + hop) % chips) + core, col) for hop in range(1, chips)] + [
         (2 * chip + mate, col),
         (2 * chip + core, 1 - col),
         (2 * chip + mate, 1 - col),
@@ -81,12 +87,24 @@
     for friend in friends:
         pl.semaphore_signal(barrier, inc=1, device_id=friend, device_id_type=MESH)
 
-    load_p.wait()
-    for block in range(4):
-        rows = slice(block * width // 2, (block + 1) * width // 2)
-        high, low = halves(p_v[:, rows].T)
-        p_high[rows, :] = high
-        p_low[rows, :] = low
+    def turn_p(panel):
+        load_p(panel).wait()
+        for block in (2 * panel, 2 * panel + 1):
+            rows = slice(block * width // 2, (block + 1) * width // 2)
+            high, low = halves(p_v[:, rows].T)
+            p_high[rows, :] = high
+            p_low[rows, :] = low
+
+    def turn_rest():
+        load_cot.wait()
+        load_inv.wait()
+        for panel in (0, 1):
+            cot_t[panel] = adj_v[:, panel * width:(panel + 1) * width].T
+            high, low = halves(inv_v[panel].T)
+            inv_high[panel] = high
+            inv_low[panel] = low
+
+    turn_p(0)
 
     def pair_copy(panel, way, step):
         return pltpu.make_async_remote_copy(
@@ -110,21 +128,23 @@
             device_id_type=MESH,
         )
 
-    def end_copy(panel, way, plane, source_core):
-        return pltpu.make_async_remote_copy(
-            terms.at[panel, way, chips - 1, source_core],
-            final.at[panel, way, source_core],
-            end_send.at[panel, way, plane],
-            end_recv.at[panel, way, source_core],
-            device_id=(2 * chip + col, jnp.where(plane == 0, col, 1 - col)),
-            device_id_type=MESH,
-        )
-
-    def end_local(panel, way, source_core):
+    def end_copy(panel, way, plane, source_core, sub):
+        rows = pl.ds(sub * piece, piece)
+        return pltpu.make_async_remote_copy(
+            terms.at[panel, way, chips - 1, source_core, rows],
+            final.at[panel, way, source_core, rows],
+            end_send.at[panel, way, plane, sub],
+            end_recv.at[panel, way, source_core, sub],
+            device_id=(2 * chip + col, col if plane == 0 else 1 - col),
+            device_id_type=MESH,
+        )
+
+    def end_local(panel, way, source_core, sub):
+        rows = pl.ds(sub * piece, piece)
         return pltpu.make_async_copy(
-            terms.at[panel, way, chips - 1, source_core],
-            final.at[panel, way, source_core],
-            end_recv.at[panel, way, source_core],
+            terms.at[panel, way, chips - 1, source_core, rows],
+            final.at[panel, way, source_core, rows],
+            end_recv.at[panel, way, source_core, sub],
         )
 
     def make_terms(count):
@@ -172,37 +192,86 @@
                 def _():
                     ring_copy(panel, way, step, sub).start()
 
-        @pl.when(step == chips - 1)
-        def _():
-            for way in (0, 1):
-                end_copy(panel, way, 1, core).start()
-
-                @pl.when(core == col)
-                def _():
-                    end_local(panel, way, core).start()
-
-                @pl.when(core != col)
-                def _():
-                    end_copy(panel, way, 0, core).start()
+                @pl.when(step == chips - 1)
+                def _():
+                    end_copy(panel, way, 1, core, sub).start()
+
+                @pl.when((step == chips - 1) & (core == col))
+                def _():
+                    end_local(panel, way, core, sub).start()
+
+                @pl.when((step == chips - 1) & (core != col))
+                def _():
+                    end_copy(panel, way, 0, core, sub).start()
+
+    side = pl.ds(pl.multiple_of(col * (width // 2), width // 2), width // 2)
+    short = width // (2 * chips)
+
+    def mate_copy(panel):
+        return pltpu.make_async_remote_copy(
+            diag_v.at[panel, :, mate],
+            diag_mate.at[panel],
+            mate_sems.at[0, panel],
+            mate_sems.at[1, panel],
+            device_id=(2 * chip + mate, col),
+            device_id_type=MESH,
+        )
+
+    def part_copy(panel, source, target):
+        return pltpu.make_async_remote_copy(
+            diag_v.at[panel, target, core],
+            diag_parts.at[panel, source],
+            part_send.at[panel, target],
+            part_recv.at[panel, source],
+            device_id=(2 * target + core, col),
+            device_id_type=MESH,
+        )
+
+    def swap_copy(panel):
+        return pltpu.make_async_remote_copy(
+            diag_out.at[panel, :, side],
+            diag_out.at[panel, :, side],
+            swap_sems.at[0, panel],
+            swap_sems.at[1, panel],
+            device_id=(2 * chip + core, 1 - col),
+            device_id_type=MESH,
+        )
+
+    def adjoint_out(panel):
+        columns = slice(panel * width, (panel + 1) * width)
+        return pltpu.make_async_copy(adj_v.at[:, columns], adjoint.at[:, columns], out_sems.at[panel])
 
     def finish(panel):
         for way in (0, 1):
             for source in (0, 1):
-                end_local(panel, way, source).wait()
-        columns = slice(panel * width, (panel + 1) * width)
-        coupled = final[panel].reshape(width, width)
-        combined = cot_v[:, columns].T - 2.0 * coupled
-        turned = product(halves(inv_v[panel].T), halves(combined))
-        adj_v[:, columns] = turned.T
-        own = (p_v[:, columns])
-        diag_v[panel] = -product(halves(turned), halves(own))
-        pltpu.make_async_copy(adj_v.at[:, columns], adjoint.at[:, columns], out_sems.at[0, panel]).start()
-        pltpu.make_async_copy(diag_v.at[panel], diag.at[panel], out_sems.at[1, panel]).start()
+                for sub in range(SUBS):
+                    end_local(panel, way, source, sub).wait()
+        combined = cot_t[panel] - 2.0 * final[panel].reshape(width, width)
+        turned = product((inv_high[panel], inv_low[panel]), halves(combined))
+        start = pl.multiple_of(panel * width + col * (width // 2), width // 2)
+        own = p_v[:, pl.ds(start, width // 2)]
+        diag_v[panel] = -product(halves(turned), halves(own)).reshape(chips, 2, short, width // 2)
+        mate_copy(panel).start()
+        adj_v[:, panel * width:(panel + 1) * width] = turned.T
+        adjoint_out(panel).start()
+
+    def scatter(panel):
+        mate_copy(panel).wait_recv()
+        diag_v[panel, :, core] = diag_v[panel, :, core] + diag_mate[panel]
+        for hop in range(1, chips):
+            part_copy(panel, chip, (chip + hop) % chips).start()
+
+    def collect(panel):
+        total = diag_v[panel, chip, core]
+        for hop in range(1, chips):
+            source = (chip + hop) % chips
+            part_copy(panel, source, chip).wait_recv()
+            total = total + diag_parts[panel, source]
+        diag_out[panel, :, side] = total
+        swap_copy(panel).start()
 
     pl.semaphore_wait(barrier, len(friends))
     make_terms(jnp.int32(0))
-    load_cot.wait()
-    load_inv.wait()
 
     def body(count, carry):
         @pl.when(count < 2 * chips - 1)
@@ -211,14 +280,29 @@
 
         ring_step(count)
 
+        @pl.when(count == 2)
+        def _():
+            turn_p(1)
+            turn_rest()
+
         @pl.when(count == chips + 2)
         def _():
             finish(0)
 
+        @pl.when(count == chips + 3)
+        def _():
+            scatter(0)
+
+        @pl.when(count == chips + 5)
+        def _():
+            collect(0)
+
         return carry
 
     lax.fori_loop(0, 2 * chips, body, 0)
     finish(1)
+    scatter(1)
+    collect(1)
 
     def drain(count, carry):
         panel, step = count // chips, count % chips
@@ -234,16 +318,22 @@
 
     lax.fori_loop(0, 2 * chips, drain, 0)
     for panel in (0, 1):
-        columns = slice(panel * width, (panel + 1) * width)
         for way in (0, 1):
-            end_copy(panel, way, 1, core).wait_send()
-
-            @pl.when(core != col)
-            def _():
-                end_copy(panel, way, 0, core).wait_send()
-
-        pltpu.make_async_copy(adj_v.at[:, columns], adjoint.at[:, columns], out_sems.at[0, panel]).wait()
-        pltpu.make_async_copy(diag_v.at[panel], diag.at[panel], out_sems.at[1, panel]).wait()
+            for sub in range(SUBS):
+                end_copy(panel, way, 1, core, sub).wait_send()
+
+                @pl.when(core != col)
+                def _():
+                    end_copy(panel, way, 0, core, sub).wait_send()
+
+        mate_copy(panel).wait_send()
+        for hop in range(1, chips):
+            part_copy(panel, chip, (chip + hop) % chips).wait_send()
+        swap_copy(panel).wait()
+        adjoint_out(panel).wait()
+    store = pltpu.make_async_copy(diag_out, diag, out_sems.at[2])
+    store.start()
+    store.wait()
 
 
 def ring_device(gbar, panels, panel_cot, inverses):
@@ -256,42 +346,51 @@
     def kernel(*refs):
         ring_kernel(chips, *refs)
 
-    adjoint, diag_terms = pl.pallas_call(
+    short = width // (2 * chips)
+    bf16 = jnp.bfloat16
+    return pl.pallas_call(
         kernel,
         out_shape=(
             jax.ShapeDtypeStruct(panels.shape, f32),
-            jax.ShapeDtypeStruct(inverses.shape, f32),
+            jax.ShapeDtypeStruct((2, short, width), f32),
         ),
         in_specs=[anywhere] * 4,
         out_specs=(anywhere, anywhere),
         scratch_shapes=[
             pltpu.VMEM((chips, width, width), f32),
             pltpu.VMEM(panels.shape, f32),
-            pltpu.VMEM(panels.shape, f32),
             pltpu.VMEM(inverses.shape, f32),
-            pltpu.VMEM((2 * width, width), jnp.bfloat16),
-            pltpu.VMEM((2 * width, width), jnp.bfloat16),
+            pltpu.VMEM(inverses.shape, f32),
+            pltpu.VMEM(inverses.shape, bf16),
+            pltpu.VMEM(inverses.shape, bf16),
+            pltpu.VMEM((2 * width, width), bf16),
+            pltpu.VMEM((2 * width, width), bf16),
             pltpu.VMEM((2, 2, chips, 2, lane, width), f32),
             pltpu.VMEM((2, 2, chips, lane, width), f32),
             pltpu.VMEM((2, 2, chips - 1, lane, width), f32),
             pltpu.VMEM((2, 2, 2, lane, width), f32),
             pltpu.VMEM(panels.shape, f32),
-            pltpu.VMEM(inverses.shape, f32),
-            dma((chips + 3,)),
-            dma((2, 2)),
+            pltpu.VMEM((2, chips, 2, short, width // 2), f32),
+            pltpu.VMEM((2, chips, short, width // 2), f32),
+            pltpu.VMEM((2, chips, short, width // 2), f32),
+            pltpu.VMEM((2, short, width), f32),
+            dma((chips + 4,)),
+            dma((3,)),
             dma((2, 2, chips)),
             dma((2, 2, chips)),
             dma((2, 2, chips - 1, SUBS)),
             dma((2, 2, chips - 1, SUBS)),
-            dma((2, 2, 2)),
-            dma((2, 2, 2)),
+            dma((2, 2, 2, SUBS)),
+            dma((2, 2, 2, SUBS)),
+            dma((2, 2)),
+            dma((2, chips)),
+            dma((2, chips)),
+            dma((2, 2)),
         ],
         compiler_params=pltpu.CompilerParams(
             collective_id=0, has_side_effects=True, vmem_limit_bytes=62 * 1024 * 1024
         ),
     )(gbar, panels, panel_cot, inverses)
-    diag_adjoint = lax.psum_scatter(diag_terms, "row", scatter_dimension=1, tiled=True)
-    return adjoint, diag_adjoint
 
 
 def plain_device(gbar, panels, panel_cot, inverses):

time: 186 us -> 126 us (0.68)
  waiting for transfers between devices: 67.3 us -> 0 us
  Pallas kernels: 103 us -> 121 us
  between operations: 14 us -> 0.65 us
  local copies, waits for them, and re-layouts: 1.32 us -> 3.85 us
    reduce_scatter x1 -> x0, waiting for transfers between devices: 67.2 us -> none  [ring_device(): lax.psum_scatter(diag_terms, 'row', scatter_dimension=1, tiled=True)]
    pallas_call x1, Pallas kernels: 103 us -> 121 us  [ring_device(): pl.pallas_call(kernel, out_shape=(jax.ShapeDtypeStruct(panels.shape, f32)...]
    unnamed x3 -> x4, local copies, waits for them, and re-layouts: 1.32 us -> 3.85 us
  transfers between devices with their start and end apart: 1 -> 0, of which waited for: 1 -> 0; matrix products, arithmetic and copies ran while one was open for 0% -> 0% of each run, Pallas kernels for 0% -> 0%
where the time goes in v2:
time: 126 us; the launch traced here: 125 us
  Pallas kernels  121 us (96%)
  local copies, waits for them, and re-layouts  3.85 us (3%)
    pallas_call x1, Pallas kernels, ring_device(): pl.pallas_call(kernel, out_shape=(jax.ShapeDtypeStruct(panels.shape, f32)...  121 us
    unnamed x4, local copies, waits for them, and re-layouts  3.85 us

profile of v2, /device:TPU:0, one launch (start us, length us, event | category | flops | bytes accessed | tf_op | source)
XLA Modules:
  0.0 125.4 jit_solution(5992860368698812597)
XLA Ops:
  0.6 120.9 %shard_map.59 = (f32[512,1024]{1,0:T(8,128)}, f32[2,32,512]{2,1,0:T(8,128)}) custom-call(f32[512,4096]{1,0:T(8,128)} %refs_0_.1, f32[512,1024]{1,0:T(8,128)} %refs_1_.1, f32[512,1024]{1,0:T(8,128)} %refs_2_.1, f32[2,512,512]{2,1,0:T(8,128)} %refs_3_.1), custom_call_target="tpu_custom_call" | custom-call | tf_op jit(solution)/shard_map/pallas_call | solution.py:351
  121.5 0.0 copy-start
  121.5 3.2 %copy.8 = f32[512,1024]{1,0:T(8,128)} copy(f32[512,1024]{1,0:T(8,128)} %get-tuple-element.4) | data formatting | bytes 4194304
  124.7 0.0 copy-done
  124.7 0.7 copy.9
Async XLA Ops:
  121.5 3.2 %copy-start = (f32[2,32,512]{2,1,0:T(8,128)S(1)}, f32[2,32,512]{2,1,0:T(8,128)}, u32[]{:S(2)}) copy-start(f32[2,32,512]{2,1,0:T(8,128)} %get-tuple-element.5) | copy-start | bytes 393220

commit v3 on v2

--- a/solution.py
+++ b/solution.py
@@ -6,7 +6,8 @@
 from jax.sharding import PartitionSpec as P
 
 MESH = pl.DeviceIdType.MESH
-SUBS = 2
+SUBS = 4
+PARTS = 2
 
 
 def halves(value):
@@ -33,8 +34,10 @@
     mate_sems, part_send, part_recv, swap_sems,
 ):
     width = inverses.shape[-1]
-    lane = width // 4
+    lane = width // (2 * PARTS)
     piece = lane // SUBS
+    total_steps = PARTS * chips
+    block = 2 * width // PARTS
     row = lax.axis_index("row")
     col = lax.axis_index("col")
     chip = row // 2
@@ -87,22 +90,25 @@
     for friend in friends:
         pl.semaphore_signal(barrier, inc=1, device_id=friend, device_id_type=MESH)
 
-    def turn_p(panel):
-        load_p(panel).wait()
-        for block in (2 * panel, 2 * panel + 1):
-            rows = slice(block * width // 2, (block + 1) * width // 2)
-            high, low = halves(p_v[:, rows].T)
-            p_high[rows, :] = high
-            p_low[rows, :] = low
-
-    def turn_rest():
-        load_cot.wait()
-        load_inv.wait()
-        for panel in (0, 1):
-            cot_t[panel] = adj_v[:, panel * width:(panel + 1) * width].T
-            high, low = halves(inv_v[panel].T)
-            inv_high[panel] = high
-            inv_low[panel] = low
+    def turn_p(part):
+        if part % (PARTS // 2) == 0:
+            load_p(part // (PARTS // 2)).wait()
+        rows = slice(part * block, (part + 1) * block)
+        high, low = halves(p_v[:, rows].T)
+        p_high[rows, :] = high
+        p_low[rows, :] = low
+
+    def turn_cot(panel):
+        if panel == 0:
+            load_cot.wait()
+        cot_t[panel] = adj_v[:, panel * width:(panel + 1) * width].T
+
+    def turn_inv(panel):
+        if panel == 0:
+            load_inv.wait()
+        high, low = halves(inv_v[panel].T)
+        inv_high[panel] = high
+        inv_low[panel] = low
 
     turn_p(0)
 
@@ -160,7 +166,7 @@
             def _():
                 load_g(tile).wait()
 
-            rows = pl.ds(pl.multiple_of(panel * width + way * (width // 2), width // 2), width // 2)
+            rows = pl.ds(pl.multiple_of(panel * block + way * (block // 2), block // 2), block // 2)
             value = product((p_high[rows, :], p_low[rows, :]), halves(g_v[tile]))
             terms[panel, way, step, 0] = value[:lane]
             terms[panel, way, step, 1] = value[lane:]
@@ -241,18 +247,25 @@
         columns = slice(panel * width, (panel + 1) * width)
         return pltpu.make_async_copy(adj_v.at[:, columns], adjoint.at[:, columns], out_sems.at[panel])
 
-    def finish(panel):
-        for way in (0, 1):
-            for source in (0, 1):
-                for sub in range(SUBS):
-                    end_local(panel, way, source, sub).wait()
-        combined = cot_t[panel] - 2.0 * final[panel].reshape(width, width)
-        turned = product((inv_high[panel], inv_low[panel]), halves(combined))
+    def solve(panel):
+        for part in range(panel * PARTS // 2, (panel + 1) * PARTS // 2):
+            for way in (0, 1):
+                for source in (0, 1):
+                    for sub in range(SUBS):
+                        end_local(part, way, source, sub).wait()
+        coupled = final[panel * PARTS // 2:(panel + 1) * PARTS // 2].reshape(width, width)
+        turned = product((inv_high[panel], inv_low[panel]), halves(cot_t[panel] - 2.0 * coupled))
+        cot_t[panel] = turned
+
+    def diagonal(panel):
         start = pl.multiple_of(panel * width + col * (width // 2), width // 2)
         own = p_v[:, pl.ds(start, width // 2)]
-        diag_v[panel] = -product(halves(turned), halves(own)).reshape(chips, 2, short, width // 2)
+        value = -product(halves(cot_t[panel]), halves(own))
+        diag_v[panel] = value.reshape(chips, 2, short, width // 2)
         mate_copy(panel).start()
-        adj_v[:, panel * width:(panel + 1) * width] = turned.T
+
+    def give(panel):
+        adj_v[:, panel * width:(panel + 1) * width] = cot_t[panel].T
         adjoint_out(panel).start()
 
     def scatter(panel):
@@ -272,36 +285,40 @@
 
     pl.semaphore_wait(barrier, len(friends))
     make_terms(jnp.int32(0))
+    ring_step(jnp.int32(0))
+    make_terms(jnp.int32(1))
+    make_terms(jnp.int32(2))
+    second = total_steps // 2
+    chores = {
+        1: lambda: turn_p(1),
+        2: lambda: turn_cot(0),
+        3: lambda: turn_cot(1),
+        4: lambda: turn_inv(0),
+        5: lambda: turn_inv(1),
+        second + 2: lambda: solve(0),
+        second + 3: lambda: diagonal(0),
+        second + 5: lambda: give(0),
+        second + 4: lambda: scatter(0),
+        second + 6: lambda: collect(0),
+    }
 
     def body(count, carry):
-        @pl.when(count < 2 * chips - 1)
+        @pl.when(count < total_steps - 2)
         def _():
-            make_terms(count + 1)
-
-        ring_step(count)
-
-        @pl.when(count == 2)
-        def _():
-            turn_p(1)
-            turn_rest()
-
-        @pl.when(count == chips + 2)
-        def _():
-            finish(0)
-
-        @pl.when(count == chips + 3)
-        def _():
-            scatter(0)
-
-        @pl.when(count == chips + 5)
-        def _():
-            collect(0)
-
+            make_terms(count + 2)
+
+        step = count % chips
+        early = (step == chips - 1) & (count < total_steps - 1)
+        ring_step(jnp.where(early, count + 1, jnp.where(step == 0, count - 1, count)))
+        for at, chore in chores.items():
+            pl.when(count == at)(chore)
         return carry
 
-    lax.fori_loop(0, 2 * chips, body, 0)
-    finish(1)
+    lax.fori_loop(1, total_steps, body, 0)
+    solve(1)
+    diagonal(1)
     scatter(1)
+    give(1)
     collect(1)
 
     def drain(count, carry):
@@ -316,16 +333,17 @@
 
         return carry
 
-    lax.fori_loop(0, 2 * chips, drain, 0)
-    for panel in (0, 1):
+    lax.fori_loop(0, total_steps, drain, 0)
+    for part in range(PARTS):
         for way in (0, 1):
             for sub in range(SUBS):
-                end_copy(panel, way, 1, core, sub).wait_send()
+                end_copy(part, way, 1, core, sub).wait_send()
 
                 @pl.when(core != col)
                 def _():
-                    end_copy(panel, way, 0, core, sub).wait_send()
-
+                    end_copy(part, way, 0, core, sub).wait_send()
+
+    for panel in (0, 1):
         mate_copy(panel).wait_send()
         for hop in range(1, chips):
             part_copy(panel, chip, (chip + hop) % chips).wait_send()
@@ -339,7 +357,7 @@
 def ring_device(gbar, panels, panel_cot, inverses):
     width = inverses.shape[-1]
     chips = lax.axis_size("row") // 2
-    lane = width // 4
+    lane = width // (2 * PARTS)
     f32, dma = jnp.float32, pltpu.SemaphoreType.DMA
     anywhere = pl.BlockSpec(memory_space=pl.ANY)
 
@@ -365,10 +383,10 @@
             pltpu.VMEM(inverses.shape, bf16),
             pltpu.VMEM((2 * width, width), bf16),
             pltpu.VMEM((2 * width, width), bf16),
-            pltpu.VMEM((2, 2, chips, 2, lane, width), f32),
-            pltpu.VMEM((2, 2, chips, lane, width), f32),
-            pltpu.VMEM((2, 2, chips - 1, lane, width), f32),
-            pltpu.VMEM((2, 2, 2, lane, width), f32),
+            pltpu.VMEM((PARTS, 2, chips, 2, lane, width), f32),
+            pltpu.VMEM((PARTS, 2, chips, lane, width), f32),
+            pltpu.VMEM((PARTS, 2, chips - 1, lane, width), f32),
+            pltpu.VMEM((PARTS, 2, 2, lane, width), f32),
             pltpu.VMEM(panels.shape, f32),
             pltpu.VMEM((2, chips, 2, short, width // 2), f32),
             pltpu.VMEM((2, chips, short, width // 2), f32),
@@ -376,12 +394,12 @@
             pltpu.VMEM((2, short, width), f32),
             dma((chips + 4,)),
             dma((3,)),
-            dma((2, 2, chips)),
-            dma((2, 2, chips)),
-            dma((2, 2, chips - 1, SUBS)),
-            dma((2, 2, chips - 1, SUBS)),
-            dma((2, 2, 2, SUBS)),
-            dma((2, 2, 2, SUBS)),
+            dma((PARTS, 2, chips)),
+            dma((PARTS, 2, chips)),
+            dma((PARTS, 2, chips - 1, SUBS)),
+            dma((PARTS, 2, chips - 1, SUBS)),
+            dma((PARTS, 2, 2, SUBS)),
+            dma((PARTS, 2, 2, SUBS)),
             dma((2, 2)),
             dma((2, chips)),
             dma((2, chips)),

time: 126 us -> 122 us (0.968)
  Pallas kernels: 121 us -> 117 us
    pallas_call x1, Pallas kernels: 121 us -> 117 us  [ring_device(): pl.pallas_call(kernel, out_shape=(jax.ShapeDtypeStruct(panels.shape, f32)...]
where the time goes in v3:
time: 122 us
  Pallas kernels  117 us (96%)
  local copies, waits for them, and re-layouts  3.85 us (3%)
    pallas_call x1, Pallas kernels, ring_device(): pl.pallas_call(kernel, out_shape=(jax.ShapeDtypeStruct(panels.shape, f32)...  117 us
    unnamed x4, local copies, waits for them, and re-layouts  3.85 us

profile of v3, /device:TPU:0, one launch (start us, length us, event | category | flops | bytes accessed | tf_op | source)
XLA Modules:
  0.0 121.6 jit_solution(3947584780854882728)
XLA Ops:
  0.6 117.1 %shard_map.59 = (f32[512,1024]{1,0:T(8,128)}, f32[2,32,512]{2,1,0:T(8,128)}) custom-call(f32[512,4096]{1,0:T(8,128)} %refs_0_.1, f32[512,1024]{1,0:T(8,128)} %refs_1_.1, f32[512,1024]{1,0:T(8,128)} %refs_2_.1, f32[2,512,512]{2,1,0:T(8,128)} %refs_3_.1), custom_call_target="tpu_custom_call" | custom-call | tf_op jit(solution)/shard_map/pallas_call | solution.py:369
  117.7 0.0 copy-start
  117.8 3.2 %copy.8 = f32[512,1024]{1,0:T(8,128)} copy(f32[512,1024]{1,0:T(8,128)} %get-tuple-element.4) | data formatting | bytes 4194304
  120.9 0.0 copy-done
  120.9 0.7 copy.9
Async XLA Ops:
  117.7 3.2 %copy-start = (f32[2,32,512]{2,1,0:T(8,128)S(1)}, f32[2,32,512]{2,1,0:T(8,128)}, u32[]{:S(2)}) copy-start(f32[2,32,512]{2,1,0:T(8,128)} %get-tuple-element.5) | copy-start | bytes 393220
